TPU v7x, 256 devices: a whole 4x4x8 slice. The times are simulated.
256 devices in a mesh: tm: 64 (over z, y, x_hi), query: 4 (over x_lo, core).
Axes of the slice: x: 4 (x_hi: 2, x_lo: 2; x = x_hi * 2 + x_lo), y: 4, z: 8, core: 2. Of those that a mesh axis runs over, the one named last changes fastest.
Arguments:
- series: float32 [262144], P('tm'), may hold values from -6 to 6
- tail: float32 [287], replicated, may hold values from -6 to 6
- queries: float32 [8192, 288], P(('tm', 'query')), may hold values from -6 to 6
Outputs:
- profile: float32 [262144], P('tm')
- query_profile: float32 [8192], P(('tm', 'query'))
All inputs are finite; a program needn't handle non-finite values.
Results may differ from a plain program's by a relative error of at most 0.0003.
Values sent between devices are 32-bit elements; how exact they have to be, the bound alone decides.
A program may use at most 192 MiB of HBM per device.

v0:
```python
import jax
import jax.numpy as jnp
from jax import lax
from jax.sharding import PartitionSpec as P


def from_behind(value, axis, by):
    peers = lax.axis_size(axis)
    pairs = [(i, i + by) for i in range(peers) if 0 <= i + by < peers]
    return lax.ppermute(value, axis, pairs)


def normalize_rows(rows):
    mean = jnp.mean(rows, axis=1, keepdims=True)
    centered = rows - mean
    sigma = jnp.sqrt(jnp.mean(centered * centered, axis=1, keepdims=True) + 1e-05)
    return centered / sigma


def window_matrix(extended, count, width):
    length = count + width
    padded = jnp.concatenate([extended, jnp.zeros((1,), jnp.float32)])
    tiled = jnp.concatenate([jnp.tile(padded, width), jnp.zeros((width,), jnp.float32)])
    windows = tiled.reshape(width, length + 1)[:, :count]
    mean = jnp.mean(windows, axis=0, keepdims=True)
    centered = windows - mean
    sigma = jnp.sqrt(jnp.mean(centered * centered, axis=0, keepdims=True) + 1e-05)
    return centered / sigma


def local(series, tail, queries):
    count = series.shape[0]
    width = queries.shape[1]
    own_rows = queries.shape[0]
    slabs = lax.axis_size("tm")
    zq = normalize_rows(queries)
    after = from_behind(series[: width - 1], "tm", -1)
    after = jnp.where(lax.axis_index("tm") == slabs - 1, tail, after)
    zt = window_matrix(jnp.concatenate([series, after]), count, width)
    pos_best = jnp.full((count,), 8.0, jnp.float32)
    scores = jnp.dot(
        lax.all_gather(zq, "tm", axis=0, tiled=True), zt, precision=lax.Precision.HIGHEST
    )
    value = 2.0 - 2.0 * scores / width
    pos_best = jnp.minimum(pos_best, jnp.min(value, axis=0))
    query_best = jnp.min(value, axis=1)
    pos_best, query_best = (pos_best, query_best)
    returned = lax.all_to_all(
        query_best.reshape(slabs, own_rows), "tm", split_axis=0, concat_axis=0, tiled=True
    )
    own_query = jnp.min(returned, axis=0)
    pos_all = lax.pmin(pos_best, "query")
    return (jnp.sqrt(pos_all), jnp.sqrt(own_query))


def solution(mesh):
    return jax.shard_map(
        local,
        mesh=mesh,
        in_specs=(P("tm"), P(), P(("tm", "query"), None)),
        out_specs=(P("tm"), P(("tm", "query"))),
        check_vma=False,
    )
```

profile of v0, /device:TPU:1, one launch (start us, length us, event | category | flops | bytes accessed | tf_op | source)
XLA Modules:
  0.0 221.8 jit_solution(16092434369876079445)
XLA Ops:
  7.2 0.0 all-gather.2.cloned.1.call-start
  7.2 0.9 reduce_sum.36
  8.1 1.0 multiply_reduce_fusion.1
  9.1 1.5 subtract_divide_fusion
  10.6 0.0 all-gather.2.cloned.1.call-update
  10.6 0.7 slice.6
  11.3 1.3 collective-permute-start
  12.6 5.1 %collective-permute-done = f32[287]{0:T(512)S(1)} collective-permute-done((f32[287]{0:T(512)S(1)}, f32[287]{0:T(512)S(1)}, u32[]{:S(2)}, u32[]{:S(2)}) %collective-permute-start) | collective-permute-done | bytes 1180 | tf_op jit(solution)/shard_map/ppermute | solution.py:10
  17.8 0.8 concatenate.6
  18.6 2.7 %tile.4 = f32[288,4384]{1,0:T(8,128)} broadcast(f32[4384]{0:T(1024)S(1)} %concatenate.6), dimensions={1} | broadcast | bytes 5067904 | tf_op jit(solution)/shard_map/tile | solution.py:23
  21.3 7.6 %tile.10 = f32[1262592]{0:T(1024)} reshape(f32[288,4384]{1,0:T(8,128)} %tile.4) | data formatting | bytes 10100736 | tf_op jit(solution)/shard_map/tile | solution.py:23
  28.9 4.2 %concatenate.7 = f32[1262880]{0:T(1024)} pad(f32[1262592]{0:T(1024)} %tile.10, f32[]{:T(128)} %constant.12.clone.1), padding=0_288 | pad | bytes 10101892 | tf_op jit(solution)/shard_map/concatenate | solution.py:23
  33.0 8.4 %reshape.36 = f32[288,4385]{1,0:T(8,128)} reshape(f32[1262880]{0:T(1024)} %concatenate.7) | data formatting | bytes 10103040 | tf_op jit(solution)/shard_map/reshape | solution.py:24
  41.5 2.6 %slice_reduce_fusion = f32[4096]{0:T(1024)S(1)} fusion(f32[288,4385]{1,0:T(8,128)} %reshape.36), kind=kLoop, calls=%fused_computation.7 | loop fusion | flops 1175552 | bytes 4734976 | tf_op jit(solution)/shard_map/reduce_sum | solution.py:25
  44.1 2.9 %multiply_reduce_fusion = f32[4096]{0:T(1024)S(1)} fusion(f32[288,4385]{1,0:T(8,128)} %reshape.36, f32[4096]{0:T(1024)S(1)} %broadcast_multiply_fusion), kind=kLoop, calls=%fused_computation.5 | loop fusion | flops 3534848 | bytes 4751360 | tf_op jit(solution)/shard_map/reduce_sum | solution.py:27
  47.0 87.9 %all-gather.2.cloned.1.call-done = f32[2048,288]{1,0:T(8,128)} async-done(((f32[32,288]{1,0:T(8,128)}), f32[2048,288]{1,0:T(8,128)}) %all-gather.2.cloned.1.call-update) | async-done | bytes 2359312 | tf_op jit(solution)/shard_map/all_gather | solution.py:42
  134.9 56.9 %fusion = (f32[2048]{0:T(1024)S(1)}, f32[4096]{0:T(1024)S(1)}) fusion(f32[2048,288]{1,0:T(8,128)} %all-gather.2.cloned.1.call-done, f32[288,4385]{1,0:T(8,128)} %reshape.36, f32[4096]{0:T(1024)S(1)} %add_sqrt_fusion, f32[4096]{0:T(1024)S(1)} %broadcast_multiply_fusion), kind=kOutput, calls=%fused_computation.1 | convolution fusion | flops 29026936832 | bytes 7921664 | tf_op jit(solution)/shard_map/dot_general | solution.py:41
  191.8 0.7 all_to_all.6
  192.5 8.1 %all-to-all-start = ((f32[64,1,32]{2,1,0:T(1,128)}), f32[64,1,32]{2,1,0:T(1,128)S(1)}, u32[]{:S(2)}, u32[]{:S(2)}) async-start(f32[64,1,32]{2,1,0:T(1,128)} %bitcast), calls=%async_computation | async-start | bytes 65536 | tf_op jit(solution)/shard_map/all_to_all | solution.py:48
  200.6 13.1 %pmin.7 = f32[4096]{0:T(1024)S(1)} all-reduce(f32[4096]{0:T(1024)S(1)} %broadcast_minimum_fusion), channel_id=1, replica_groups=mesh['tm'=64,'query'=4] {'query'}, use_global_device_ids=true, to_apply=%region_5.6 | all-reduce | flops 4096 | bytes 32768 | tf_op jit(solution)/shard_map/pmin | solution.py:52
  213.7 0.6 sqrt.24
  214.3 0.0 all-to-all-done
  214.3 0.1 reduce_min.29
  214.4 0.5 sqrt.25
  (6 shorter events, 0.0 us)
Async XLA Ops:
  7.2 127.7 %all-gather.2.cloned.1.call-start = ((), (), s32[]{:S(2)}) async-start(), calls=%async_computation.1 | async-start | bytes 3194880 | tf_op jit(solution)/shard_map/all_gather | solution.py:42
  11.3 6.4 %collective-permute-start = (f32[287]{0:T(512)S(1)}, f32[287]{0:T(512)S(1)}, u32[]{:S(2)}, u32[]{:S(2)}) collective-permute-start(f32[287]{0:T(512)S(1)} %slice.6), channel_id=1, source_target_pairs={{4,0},{8,4},{12,8},{16,12},{20,16},{24,20},{28,24},{32,28},{36,32}... | collective-permute-start | bytes 3452 | tf_op jit(solution)/shard_map/ppermute | solution.py:10
  192.5 21.9 %all-to-all-start = ((f32[64,1,32]{2,1,0:T(1,128)}), f32[64,1,32]{2,1,0:T(1,128)S(1)}, u32[]{:S(2)}, u32[]{:S(2)}) async-start(f32[64,1,32]{2,1,0:T(1,128)} %bitcast), calls=%async_computation | async-start | bytes 65536 | tf_op jit(solution)/shard_map/all_to_all | solution.py:48
Sparse Core Ops, SparseCore 0:
  11.5 123.2 all-gather.1
where the time goes:
time: 223 us; the launch traced here: 222 us
  waiting for transfers between devices  93.1 us (42%)
  matrix products  56.9 us (26%)
  local copies, waits for them, and re-layouts  26.2 us (12%)
  between operations  14.1 us (6%)
  blocking collectives  13.1 us (6%)
  starting transfers between devices  9.42 us (4%)
  other arithmetic  8.98 us (4%)
    all_gather x1, waiting for transfers between devices, local(): lax.all_gather(zq, 'tm', axis=0, tiled=True)  87.9 us
    dot_general x1, matrix products, local(): jnp.dot(lax.all_gather(zq, 'tm', axis=0, tiled=True), zt, precision=lax.P...  56.9 us
    pmin x1, blocking collectives, local(): pos_all = lax.pmin(pos_best, 'query')  13.1 us
    another operation x2, local copies, waits for them, and re-layouts, window_matrix(): jnp.tile(padded, width)  10.3 us
    reshape x1, local copies, waits for them, and re-layouts, window_matrix(): windows = tiled.reshape(width, length + 1)[:, :count]  8.42 us
    all_to_all x1, starting transfers between devices, local(): lax.all_to_all(query_best.reshape(slabs, own_rows), 'tm', split_axis=0, c...  8.1 us
    ppermute x1, waiting for transfers between devices, from_behind(): return lax.ppermute(value, axis, pairs)  5.14 us
  transfers between devices with their start and end apart: 3, of which 2 were waited for; matrix products, arithmetic and copies ran while one was open for 14% of the time, Pallas kernels for 0%

commit v1 on v0

v1 whole, which is shorter than its diff:
```python
import jax
import jax.numpy as jnp
from jax import lax
from jax.experimental import pallas as pl
from jax.experimental.pallas import tpu as pltpu
from jax.sharding import PartitionSpec as P

M = 288
SEG = 1024
LANES = 128
COLUMN = 32
GROUP = 8
REPLICAS = 4
REST = M - 256
MESH = pl.DeviceIdType.MESH


def split(value):
    high = value.astype(jnp.bfloat16)
    low = (value - high.astype(jnp.float32)).astype(jnp.bfloat16)
    return high, low


def hankel(row, blocks):
    r = lax.broadcasted_iota(jnp.int32, (LANES, LANES), 0)
    lane = lax.broadcasted_iota(jnp.int32, (LANES, LANES), 1)
    this = pltpu.roll(jnp.broadcast_to(row(0), (LANES, LANES)), 1, 1, stride=1, stride_axis=0)
    for u in range(blocks):
        after = pltpu.roll(jnp.broadcast_to(row(u + 1), (LANES, LANES)), 1, 1, stride=1, stride_axis=0)
        yield u, jnp.where(lane <= r, this, after)
        this = after


def kernel(
    series, tail, queries, prof, qprof,
    ext, halo, own_h, segs, bha, bla, bhb, blb, zall, zcat, acc, part, got, qpart, qgot, pall,
    halo_s, halo_r, zs, zr, ss, sr, ps, pr, qs, qr, fs, fr,
):
    tm, q = lax.axis_index("tm"), lax.axis_index("query")
    zz, yy, xh = tm // 8, (tm // 2) % 4, tm % 2
    gidx = xh * 4 + q

    def col(s, sign):
        z2 = (zz + sign * (s // 4) + 8) % 8
        y2 = (yy + sign * (s % 4) + 4) % 4
        return (z2 * 8 + y2 * 2 + xh, q)

    def grp(j, sign):
        g = (gidx + sign * j + 8) % 8
        return (tm - xh + g // 4, g % 4)

    def rep(j, sign):
        return (tm, (q + sign * j + 4) % 4)

    def remote(src, dst, send, recv, device):
        return pltpu.make_async_remote_copy(
            src_ref=src, dst_ref=dst, send_sem=send, recv_sem=recv, device_id=device, device_id_type=MESH
        )

    def halo_copy():
        return remote(series.at[0:8], halo, halo_s.at[0], halo_r.at[0], ((tm + 63) % 64, q))

    def z_copy(j):
        return remote(zall.at[0], zall.at[j], zs.at[j], zr.at[j], grp(j, 1))

    def seg_copy(s):
        return remote(segs.at[0], segs.at[s], ss.at[s], sr.at[s], col(s, 1))

    def part_copy(s):
        return remote(part.at[s], got.at[s], ps.at[s], pr.at[s], col(s, -1))

    def q_copy(j):
        return remote(qpart.at[j // 4], qgot.at[j], qs.at[j], qr.at[j], grp(j, -1))

    def final_copy(j):
        return remote(pall.at[0], pall.at[j], fs.at[j], fr.at[j], rep(j, 1))

    def each(low, high, do):
        lax.fori_loop(low, high, lambda i, c: (do(i), c)[1], 0)

    barrier = pltpu.get_barrier_semaphore()

    def hello(device):
        pl.semaphore_signal(barrier, inc=1, device_id=device, device_id_type=MESH)

    hello(((tm + 1) % 64, q))
    each(1, GROUP, lambda j: hello(grp(j, 1)))
    each(1, COLUMN, lambda s: hello(col(s, 1)))

    rows = queries[...]
    centered = rows - jnp.mean(rows, axis=1, keepdims=True)
    sigma = jnp.sqrt(jnp.mean(centered * centered, axis=1, keepdims=True) + 1e-05)
    zq = centered / sigma
    k = lax.broadcasted_iota(jnp.int32, (M, 384), 0)
    c = lax.broadcasted_iota(jnp.int32, (M, 384), 1)
    source = jnp.where(
        c < 128, 127 - c, jnp.where(c < 256, 383 - c, jnp.where(c < 352, 287 - c % REST, -1))
    )
    place = (k == source).astype(jnp.float32)
    zp = jnp.dot(zq, place, precision=lax.Precision.HIGHEST, preferred_element_type=jnp.float32)
    high, low = split(zp)
    kept = high.astype(jnp.float32) + low.astype(jnp.float32)
    lane = lax.broadcasted_iota(jnp.int32, (32, 384), 1)
    excess = jnp.sum(jnp.where(lane < M, kept, 0.0), axis=1, keepdims=True)
    zall[0] = jnp.where(lane < 352, zp, excess * (-1.0 / REST))
    acc[...] = jnp.full_like(acc, -1e30)
    ext[0:32] = series[...]

    pl.semaphore_wait(barrier, 1 + (GROUP - 1) + (COLUMN - 1))
    halo_copy().start()
    each(1, GROUP, lambda j: z_copy(j).start())
    halo_copy().wait_recv()
    ext[32:40] = jnp.where(tm == 63, tail[...], halo[...])

    x = ext[pl.ds(pl.multiple_of(q * 8, 8), 16)]
    segs[0, 0:16] = x - jnp.mean(x[0:8])
    for u, block in hankel(lambda i: segs[0, i : i + 1], 10):
        own_h[:, u * LANES : (u + 1) * LANES] = block
    for u in range(8):
        blocks = [own_h[:, (u + b) * LANES : (u + b + 1) * LANES] for b in (0, 1)]
        blocks.append(own_h[LANES - REST :, (u + 2) * LANES : (u + 3) * LANES])
        mean = sum(jnp.sum(b, axis=0, keepdims=True) for b in blocks) / M
        var = sum(jnp.sum((b - mean) * (b - mean), axis=0, keepdims=True) for b in blocks) / M
        segs[0, 16 + u : 17 + u] = 1.0 / jnp.sqrt(var + 1e-05)
    each(1, COLUMN, lambda s: seg_copy(s).start())

    def build(s, bh, bl, i):
        for u, block in hankel(lambda n: segs[s, n : n + 1], 10):
            bh[i, :, u * LANES : (u + 1) * LANES], bl[i, :, u * LANES : (u + 1) * LANES] = split(block)

    def compute(s, bh, bl, i):
        for t in range(SEG // 256):
            p = t * 256

            def two(ref):
                return [ref[i, :, p : p + 256], ref[i, :, p + 128 : p + 384]]

            def rest(ref):
                return ref[i, LANES - REST :, p + 256 : p + 512]

            h = jnp.concatenate(two(bh) + two(bh) + two(bl) + [rest(bh), rest(bh), rest(bl), rest(bh)], axis=0)
            out = jnp.dot(zcat[...], h, preferred_element_type=jnp.float32)
            best = jnp.max(out.reshape(32, 8, 256), axis=0)
            left = out[:, :LANES] * segs[s, 16 + 2 * t : 17 + 2 * t]
            right = out[:, LANES:] * segs[s, 17 + 2 * t : 18 + 2 * t]
            acc[...] = jnp.maximum(acc[...], jnp.maximum(left, right))
            part[s, 2 * t : 2 * t + 1] = jnp.max(best[:, :LANES], axis=0, keepdims=True)
            part[s, 2 * t + 1 : 2 * t + 2] = jnp.max(best[:, LANES:], axis=0, keepdims=True)

    build(0, bha, bla, 0)
    seg_copy(1).wait_recv()
    build(1, bha, bla, 1)

    each(1, GROUP, lambda j: z_copy(j).wait_recv())
    for j in range(GROUP):
        at = slice(32 * j, 32 * j + 32)
        value = zall[j]
        high, low = split(value)
        zcat[at, 0:256] = high[:, :256]
        zcat[at, 256:512] = low[:, :256]
        zcat[at, 512:768] = high[:, :256]
        four = lax.broadcasted_iota(jnp.int32, (32, LANES), 1)
        second = (four >= REST) & (four < 2 * REST)
        mixed = jnp.where(second, low[:, 256:].astype(jnp.float32), high[:, 256:].astype(jnp.float32))
        zcat[at, 768:896] = mixed.astype(jnp.bfloat16)

    def step(i, carry):
        s = 4 * i
        seg_copy(s + 2).wait_recv()
        seg_copy(s + 3).wait_recv()

        @pl.when(i < 7)
        def _():
            seg_copy(s + 4).wait_recv()
            seg_copy(s + 5).wait_recv()

        compute(s, bha, bla, 0)
        build(s + 2, bhb, blb, 0)
        compute(s + 1, bha, bla, 1)
        build(s + 3, bhb, blb, 1)
        compute(s + 2, bhb, blb, 0)
        build(jnp.minimum(s + 4, 30), bha, bla, 0)
        compute(s + 3, bhb, blb, 1)
        build(jnp.minimum(s + 5, 31), bha, bla, 1)

        @pl.when(i > 0)
        def _():
            part_copy(s).start()

        for n in (1, 2, 3):
            part_copy(s + n).start()
        return carry

    lax.fori_loop(0, COLUMN // 4, step, 0)

    best = jnp.max(jnp.transpose(acc[...]), axis=0, keepdims=True)
    qpart[0] = jnp.broadcast_to(best[:, :LANES], (8, LANES))
    qpart[1] = jnp.broadcast_to(best[:, LANES:], (8, LANES))
    each(1, GROUP, lambda j: q_copy(j).start())

    def distance(product):
        return jnp.sqrt(jnp.maximum(2.0 - 2.0 * product / M, 0.0))

    def fold(s, best):
        part_copy(s).wait_recv()
        return jnp.maximum(best, got[s])

    own = lax.fori_loop(1, COLUMN, fold, part[0])
    pall[0] = distance(own * segs[0, 16:24])
    each(1, REPLICAS, lambda j: final_copy(j).start())

    own = qpart[0, 0:1, 0:32]
    for j in range(1, GROUP):
        q_copy(j).wait_recv()
        own = jnp.maximum(own, qgot[j, 0:1, 32 * (j % 4) : 32 * (j % 4) + 32])
    qprof[...] = distance(own)

    for j in range(REPLICAS):
        if j:
            final_copy(j).wait_recv()
        at = pl.multiple_of(((q - j + 4) % 4) * 8, 8)
        prof[pl.ds(at, 8)] = pall[j]

    halo_copy().wait_send()
    each(1, GROUP, lambda j: z_copy(j).wait_send())
    each(1, COLUMN, lambda s: seg_copy(s).wait_send())
    each(1, COLUMN, lambda s: part_copy(s).wait_send())
    each(1, GROUP, lambda j: q_copy(j).wait_send())
    each(1, REPLICAS, lambda j: final_copy(j).wait_send())


def local(series, tail, queries):
    f32, bf16, dma = jnp.float32, jnp.bfloat16, pltpu.SemaphoreType.DMA
    vmem = pl.BlockSpec(memory_space=pltpu.VMEM)
    prof, qprof = pl.pallas_call(
        kernel,
        out_shape=[jax.ShapeDtypeStruct((32, LANES), f32), jax.ShapeDtypeStruct((1, 32), f32)],
        in_specs=[vmem] * 3,
        out_specs=[vmem] * 2,
        scratch_shapes=[
            pltpu.VMEM((40, LANES), f32),
            pltpu.VMEM((8, LANES), f32),
            pltpu.VMEM((LANES, 1280), f32),
            pltpu.VMEM((COLUMN, 24, LANES), f32),
            pltpu.VMEM((2, LANES, 1280), bf16),
            pltpu.VMEM((2, LANES, 1280), bf16),
            pltpu.VMEM((2, LANES, 1280), bf16),
            pltpu.VMEM((2, LANES, 1280), bf16),
            pltpu.VMEM((GROUP, 32, 384), f32),
            pltpu.VMEM((256, 896), bf16),
            pltpu.VMEM((256, LANES), f32),
            pltpu.VMEM((COLUMN, 8, LANES), f32),
            pltpu.VMEM((COLUMN, 8, LANES), f32),
            pltpu.VMEM((2, 8, LANES), f32),
            pltpu.VMEM((GROUP, 8, LANES), f32),
            pltpu.VMEM((REPLICAS, 8, LANES), f32),
            dma((1,)), dma((1,)),
            dma((GROUP,)), dma((GROUP,)),
            dma((COLUMN,)), dma((COLUMN,)),
            dma((COLUMN,)), dma((COLUMN,)),
            dma((GROUP,)), dma((GROUP,)),
            dma((REPLICAS,)), dma((REPLICAS,)),
        ],
        compiler_params=pltpu.CompilerParams(
            collective_id=0, has_side_effects=True, vmem_limit_bytes=40 * 2**20
        ),
    )(series.reshape(32, LANES), jnp.pad(tail, (0, 1024 - tail.shape[0])).reshape(8, LANES), queries)
    return prof.reshape(4096), qprof.reshape(32)


def solution(mesh):
    return jax.shard_map(
        local,
        mesh=mesh,
        in_specs=(P("tm"), P(), P(("tm", "query"), None)),
        out_specs=(P("tm"), P(("tm", "query"))),
        check_vma=False,
    )
```

time: 223 us -> 53.3 us (0.24)
  waiting for transfers between devices: 93.1 us -> 0 us
  matrix products: 56.9 us -> 0 us
  Pallas kernels: 0 us -> 49.1 us
  local copies, waits for them, and re-layouts: 26.2 us -> 3.32 us
  between operations: 14.1 us -> 0.64 us
  blocking collectives: 13.1 us -> 0 us
  starting transfers between devices: 9.42 us -> 0 us
  other arithmetic: 8.98 us -> 0 us
    all_gather x1 -> x0, waiting for transfers between devices: 87.9 us -> none  [local(): lax.all_gather(zq, 'tm', axis=0, tiled=True)]
    dot_general x1 -> x0, matrix products: 56.9 us -> none  [local(): jnp.dot(lax.all_gather(zq, 'tm', axis=0, tiled=True), zt, precision=lax.P...]
    pallas_call x0 -> x1, Pallas kernels: none -> 49.1 us  [local(): pl.pallas_call(kernel, out_shape=[jax.ShapeDtypeStruct((32, LANES), f32),...]
    pmin x1 -> x0, blocking collectives: 13.1 us -> none  [local(): pos_all = lax.pmin(pos_best, 'query')]
    another operation x2 -> x0, local copies, waits for them, and re-layouts: 10.3 us -> none  [window_matrix(): jnp.tile(padded, width)]
    all_to_all x1 -> x0, starting transfers between devices: 8.1 us -> none  [local(): lax.all_to_all(query_best.reshape(slabs, own_rows), 'tm', split_axis=0, c...]
    reshape x1, local copies, waits for them, and re-layouts: 8.42 us -> 0.69 us  [local(): jnp.pad(tail, (0, 1024 - tail.shape[0])).reshape(8, LANES)]
    reduce_sum x4 -> x0, other arithmetic: 7.35 us -> none  [the longest x1 2.87 us: window_matrix(): jnp.mean(centered * centered, axis=0, keepdims=True) + 1e-05]
  transfers between devices with their start and end apart: 3 -> 0, of which waited for: 2 -> 0; matrix products, arithmetic and copies ran while one was open for 14% -> 0% of each run, Pallas kernels for 0% -> 0%
where the time goes in v1:
time: 53.3 us; the launch traced here: 53.1 us
  Pallas kernels  49.1 us (92%)
  local copies, waits for them, and re-layouts  3.32 us (6%)
  between operations  0.64 us (1%)
    pallas_call x1, Pallas kernels, local(): pl.pallas_call(kernel, out_shape=[jax.ShapeDtypeStruct((32, LANES), f32),...  49.1 us
    unnamed x6, local copies, waits for them, and re-layouts  2.63 us

profile of v1, /device:TPU:1, one launch (start us, length us, event | category | flops | bytes accessed | tf_op | source)
XLA Modules:
  0.0 53.1 jit_solution(12844109174261094463)
XLA Ops:
  0.6 0.7 %pad_bitcast_fusion.tail = f32[8,128]{1,0:T(8,128)S(1)} fusion(f32[287]{0:T(512)} %param.4), kind=kLoop, calls=%fused_computation | loop fusion | bytes 5244 | tf_op jit(solution)/shard_map/reshape | solution.py:267
  1.3 0.0 copy-start
  1.3 0.8 %copy-done = f32[32,288]{1,0:T(8,128)S(1)} copy-done((f32[32,288]{1,0:T(8,128)S(1)}, f32[32,288]{1,0:T(8,128)}, u32[]{:S(2)}) %copy-start) | copy-done | bytes 36888
  2.1 0.0 copy-start.1
  2.1 0.7 %copy-done.1 = f32[4096]{0:T(1024)S(1)} copy-done((f32[4096]{0:T(1024)S(1)}, f32[4096]{0:T(1024)}, u32[]{:S(2)}) %copy-start.1) | copy-done | bytes 16408
  2.8 49.1 %shard_map.50 = (f32[32,128]{1,0:T(8,128)S(1)}, f32[1,32]{1,0:T(1,128)S(1)}) custom-call(f32[32,128]{1,0:T(8,128)S(1)} %bitcast.5, f32[8,128]{1,0:T(8,128)S(1)} %pad_bitcast_fusion.tail, f32[32,288]{1,0:T(8,128)S(1)} %copy-done), custom_call_target="tpu_custom_call" | custom-call | tf_op jit(solution)/shard_map/pallas_call | solution.py:235
  52.0 0.6 %copy.7 = f32[4096]{0:T(1024)} copy(f32[4096]{0:T(1024)S(1)} %bitcast.6) | data formatting | bytes 32768
  52.6 0.5 copy.8
Async XLA Ops:
  1.3 0.8 %copy-start = (f32[32,288]{1,0:T(8,128)S(1)}, f32[32,288]{1,0:T(8,128)}, u32[]{:S(2)}) copy-start(f32[32,288]{1,0:T(8,128)} %queries.1) | copy-start | bytes 110596
  2.1 0.7 %copy-start.1 = (f32[4096]{0:T(1024)S(1)}, f32[4096]{0:T(1024)}, u32[]{:S(2)}) copy-start(f32[4096]{0:T(1024)} %param.3) | copy-start | bytes 49156

commit v2 on v1

v2 whole, which is shorter than its diff:
```python
import jax
import jax.numpy as jnp
from jax import lax
from jax.experimental import pallas as pl
from jax.experimental.pallas import tpu as pltpu
from jax.sharding import PartitionSpec as P

M = 288
SEG = 1024
LANES = 128
COLUMN = 32
GROUP = 8
REPLICAS = 4
REST = M - 256
MESH = pl.DeviceIdType.MESH


def split(value):
    high = value.astype(jnp.bfloat16)
    low = (value - high.astype(jnp.float32)).astype(jnp.bfloat16)
    return high, low


def hankel(row, blocks):
    r = lax.broadcasted_iota(jnp.int32, (LANES, LANES), 0)
    lane = lax.broadcasted_iota(jnp.int32, (LANES, LANES), 1)
    this = pltpu.roll(jnp.broadcast_to(row(0), (LANES, LANES)), 1, 1, stride=1, stride_axis=0)
    for u in range(blocks):
        after = pltpu.roll(jnp.broadcast_to(row(u + 1), (LANES, LANES)), 1, 1, stride=1, stride_axis=0)
        yield u, jnp.where(lane <= r, this, after)
        this = after


def ahead(value, by):
    if by % LANES == 0:
        return pltpu.roll(value, 16 - by // LANES, 0)
    here = pltpu.roll(value, LANES - by, 1)
    lanes = lax.broadcasted_iota(jnp.int32, (16, LANES), 1)
    return jnp.where(lanes < LANES - by, here, pltpu.roll(here, 15, 0))


def scales(x):
    mean, dev, n = x, None, 1
    while n < 256:
        gap = ahead(mean, n) - mean
        joined = gap * gap * (n / 2)
        dev = joined if dev is None else dev + ahead(dev, n) + joined
        mean = mean + 0.5 * gap
        n *= 2
        if n == REST:
            mean_rest, dev_rest = mean, dev
    gap = ahead(mean_rest, 256) - mean
    dev = dev + ahead(dev_rest, 256) + gap * gap * (256 * REST / M)
    return 1.0 / jnp.sqrt(dev[0:8] / M + 1e-05)


def kernel(
    series, tail, queries, prof, qprof,
    ext, tail_v, rows_v, segs, bha, bla, bhb, blb, zall, zcat, acc, part, got, found, qpart, qgot, pall, last,
    ls, halo_s, halo_r, zs, zr, ss, sr, ps, pr, qs, qr, fs, fr,
):
    tm, q = lax.axis_index("tm"), lax.axis_index("query")
    zz, yy, xh = lax.div(tm, 8), lax.rem(lax.div(tm, 2), 4), lax.rem(tm, 2)
    xx, core = xh * 2 + lax.div(q, 2), lax.rem(q, 2)

    def col(s, sign):
        s = jnp.int32(s)
        z2 = lax.rem(zz + sign * lax.div(s, 4) + 8, 8)
        y2 = lax.rem(yy + sign * lax.rem(s, 4) + 4, 4)
        return (z2 * 8 + y2 * 2 + xh, q)

    def grp(j, sign):
        x2 = lax.rem(xx + sign * lax.div(j, 2) + 4, 4)
        c2 = lax.rem(core + lax.rem(j, 2), 2)
        return (tm - xh + lax.div(x2, 2), lax.rem(x2, 2) * 2 + c2)

    def rep(j, sign):
        return (tm, lax.rem(q + sign * j + 4, 4))

    def remote(src, dst, send, recv, device):
        return pltpu.make_async_remote_copy(
            src_ref=src, dst_ref=dst, send_sem=send, recv_sem=recv, device_id=device, device_id_type=MESH
        )

    def halo_copy():
        return remote(ext.at[0:8], ext.at[32:40], halo_s.at[0], halo_r.at[0], (lax.rem(tm + 63, 64), 3))

    def z_copy(j):
        return remote(zall.at[0], zall.at[j], zs.at[j], zr.at[j], grp(jnp.int32(j), 1))

    def z_forward(j):
        return remote(zall.at[j - 1], zall.at[j], zs.at[j], zr.at[j], grp(jnp.int32(1), 1))

    def seg_copy(s):
        return remote(segs.at[0], segs.at[s], ss.at[s], sr.at[s], col(s, 1))

    def part_copy(s):
        return remote(part.at[s], got.at[s], ps.at[s], pr.at[s], col(s, -1))

    def q_copy(j):
        return remote(qpart.at[j % 2], qgot.at[j], qs.at[j], qr.at[j], grp(jnp.int32(j), -1))

    def last_copy(n, j):
        device = (col(28 + n, -1)[0], lax.rem(q + j, 4))
        return remote(part.at[28 + n], last.at[4 * j + n], fs.at[4 * j + n], fr.at[4 * j + n], device)

    def final_copy(j):
        return remote(pall.at[0], pall.at[j], fs.at[16 + j], fr.at[16 + j], rep(jnp.int32(j), 1))

    def each(low, high, do):
        lax.fori_loop(low, high, lambda i, c: (do(i), c)[1], 0)

    loads = [
        pltpu.make_async_copy(queries, rows_v, ls.at[0]),
        pltpu.make_async_copy(series, ext.at[0:32], ls.at[1]),
        pltpu.make_async_copy(tail, tail_v, ls.at[2]),
    ]
    for load in loads:
        load.start()

    barrier = pltpu.get_barrier_semaphore()

    def hello(device):
        pl.semaphore_signal(barrier, inc=1, device_id=device, device_id_type=MESH)

    each(1, GROUP, lambda j: hello(grp(j, 1)))
    each(1, COLUMN, lambda s: hello(col(s, 1)))
    hello((lax.rem(tm + 1, 64), lax.rem(q + 2, 4)))
    each(0, 12, lambda i: hello((col(28 + lax.rem(i, 4), 1)[0], lax.rem(q + 1 + lax.div(i, 4), 4))))

    loads[0].wait()
    rows = rows_v[...]
    centered = rows - jnp.mean(rows, axis=1, keepdims=True)
    sigma = jnp.sqrt(jnp.mean(centered * centered, axis=1, keepdims=True) + 1e-05)
    zq = centered / sigma
    k = lax.broadcasted_iota(jnp.int32, (M, 384), 0)
    c = lax.broadcasted_iota(jnp.int32, (M, 384), 1)
    source = jnp.where(c < 128, 127 - c, jnp.where(c < 256, 383 - c, 287 - c % REST))
    place = (k == source).astype(jnp.float32)
    zp = jnp.dot(zq, place, precision=lax.Precision.HIGHEST, preferred_element_type=jnp.float32)
    lane = lax.broadcasted_iota(jnp.int32, (8, LANES), 1)
    quad = lane // REST
    packed = zp[24:32, 256:384]
    for g in range(3):
        packed = jnp.where(quad == g, zp[8 * g : 8 * g + 8, 256:384], packed)
    zall[0, 0:32] = zp[:, :128]
    zall[0, 32:64] = zp[:, 128:256]
    zall[0, 64:72] = packed
    acc[...] = jnp.full_like(acc, -1e30)
    loads[1].wait()
    loads[2].wait()

    @pl.when((q == 3) & (tm == 63))
    def _():
        ext[32:40] = jnp.zeros((8, LANES), jnp.float32)
        ext[32:33] = tail_v[0:128].reshape(1, LANES)
        ext[33:34] = tail_v[128:256].reshape(1, LANES)
        ext[34:35, 0 : REST - 1] = tail_v[256 : M - 1].reshape(1, REST - 1)

    def message():
        x = ext[pl.ds(pl.multiple_of(q * 8, 8), 16)]
        x = x - jnp.mean(x[0:8])
        segs[0, 0:16] = x
        segs[0, 16:24] = scales(x)

    @pl.when((q < 3) | (tm == 63))
    def _():
        message()

    pl.semaphore_wait(barrier, 1 + (GROUP - 1) + (COLUMN - 1) + 12)

    @pl.when((q == 1) & (tm > 0))
    def _():
        halo_copy().start()

    for j in (2, 6, 4, 1):
        z_copy(j).start()

    @pl.when((q == 3) & (tm < 63))
    def _():
        halo_copy().wait_recv()
        message()

    each(1, COLUMN, lambda s: seg_copy(s).start())

    def build(s, bh, bl, i):
        for u, block in hankel(lambda n: segs[s, n : n + 1], 10):
            bh[i, :, u * LANES : (u + 1) * LANES], bl[i, :, u * LANES : (u + 1) * LANES] = split(block)

    def compute(s, bh, bl, i, low=0, high=256):
        for t in range(SEG // 256):
            p = t * 256

            def two(ref):
                return [ref[i, :, p : p + 256], ref[i, :, p + 128 : p + 384]]

            def rest(ref):
                return ref[i, LANES - REST :, p + 256 : p + 512]

            h = jnp.concatenate(two(bh) + two(bh) + two(bl) + [rest(bh), rest(bh), rest(bl), rest(bh)], axis=0)
            out = jnp.dot(zcat[low:high], h, preferred_element_type=jnp.float32)
            best = jnp.max(out.reshape((high - low) // 8, 8, 256), axis=0)
            scaled = []
            for n in (0, 1):
                u, half = 2 * t + n, slice(n * LANES, (n + 1) * LANES)
                scale = segs[s, 16 + u : 17 + u]
                scaled.append(out[:, half] * scale)
                top = jnp.max(best[:, half], axis=0, keepdims=True) * scale
                part[s, u : u + 1] = jnp.maximum(part[s, u : u + 1], top) if low else top
            acc[low:high] = jnp.maximum(acc[low:high], jnp.maximum(*scaled))

    def take(j):
        at = slice(32 * (j // 2) + 128 * (j % 2), 32 * (j // 2) + 128 * (j % 2) + 32)
        total = jnp.zeros((32, 1), jnp.float32)
        for b in (0, 1):
            value = zall[j, 32 * b : 32 * b + 32]
            high, low = split(value)
            zcat[at, 128 * b : 128 * b + 128] = high
            zcat[at, 256 + 128 * b : 384 + 128 * b] = low
            zcat[at, 512 + 128 * b : 640 + 128 * b] = high
            total += jnp.sum(high.astype(jnp.float32) + low.astype(jnp.float32), axis=1, keepdims=True)
        four = []
        for g in range(4):
            value = jnp.where(quad == g, zall[j, 64:72], 0.0)
            value = value + pltpu.roll(value, 32, 1)
            four.append(value + pltpu.roll(value, 64, 1))
        value = jnp.concatenate(four, axis=0)
        high, low = split(value)
        high, low = high.astype(jnp.float32), low.astype(jnp.float32)
        lanes = lax.broadcasted_iota(jnp.int32, (32, LANES), 1)
        total += jnp.sum(jnp.where(lanes < REST, high + low, 0.0), axis=1, keepdims=True)
        part_of = lanes // REST
        mixed = jnp.where(part_of == 1, low, jnp.where(part_of == 3, total * (-1.0 / REST), high))
        zcat[at, 768:896] = mixed.astype(jnp.bfloat16)

    def four(s, last=False):
        for n in (2, 3) if last else (2, 3, 4, 5):
            seg_copy(s + n).wait_recv()
        compute(s, bha, bla, 0)
        build(s + 2, bhb, blb, 0)
        compute(s + 1, bha, bla, 1)
        build(s + 3, bhb, blb, 1)
        compute(s + 2, bhb, blb, 0)
        if not last:
            build(s + 4, bha, bla, 0)
        compute(s + 3, bhb, blb, 1)
        if not last:
            build(s + 5, bha, bla, 1)
        for n in range(4):
            if last:
                for j in range(REPLICAS):
                    last_copy(n, j).start()
            else:
                part_copy(s + n).start()

    def fold(s):
        part_copy(s).wait_recv()
        found[...] = jnp.maximum(found[...], got[s])

    take(0)
    build(0, bha, bla, 0)
    for j in (2, 6, 4):
        z_copy(j).wait_recv()
        z_forward(j + 1).start()
        take(j)
    compute(0, bha, bla, 0, 0, 128)
    seg_copy(1).wait_recv()
    build(1, bha, bla, 1)
    compute(1, bha, bla, 1, 0, 128)
    z_copy(1).wait_recv()
    take(1)
    for j in (3, 7, 5):
        z_forward(j).wait_recv()
        take(j)
    for n in (2, 3, 4, 5):
        seg_copy(n).wait_recv()
    compute(0, bha, bla, 0, 128, 256)
    build(2, bhb, blb, 0)
    compute(1, bha, bla, 1, 128, 256)
    build(3, bhb, blb, 1)
    compute(2, bhb, blb, 0)
    build(4, bha, bla, 0)
    compute(3, bhb, blb, 1)
    build(5, bha, bla, 1)
    for n in (1, 2, 3):
        part_copy(n).start()
    found[...] = part[0]

    def step(i, carry):
        s = 8 * i + 4
        four(s)
        four(s + 4)

        return carry

    lax.fori_loop(0, 3, step, 0)
    four(28, last=True)

    best = jnp.max(jnp.transpose(acc[...]), axis=0, keepdims=True)
    qpart[0] = jnp.broadcast_to(best[:, :LANES], (8, LANES))
    qpart[1] = jnp.broadcast_to(best[:, LANES:], (8, LANES))
    for j in range(1, GROUP):
        q_copy(j).start()

    def distance(product):
        return jnp.sqrt(jnp.maximum(2.0 - 2.0 * product / M, 0.0))

    for n in range(1, 28):
        fold(n)
    pall[0] = found[...]
    for j in range(1, REPLICAS):
        final_copy(j).start()

    own = qpart[0, 0:1, 0:32]
    for j in range(1, GROUP):
        q_copy(j).wait_recv()
        own = jnp.maximum(own, qgot[j, 0:1, 32 * (j // 2) : 32 * (j // 2) + 32])
    qprof[...] = distance(own)

    for j in range(REPLICAS):
        for n in range(4):
            last_copy(n, j).wait_recv()
        if j:
            final_copy(j).wait_recv()
        best = jnp.maximum(pall[j], jnp.max(last[4 * j : 4 * j + 4], axis=0))
        at = pl.multiple_of(lax.rem(q - j + 4, 4) * 8, 8)
        prof[pl.ds(at, 8)] = distance(best)

    @pl.when((q == 1) & (tm > 0))
    def _():
        halo_copy().wait_send()

    for j in range(1, GROUP):
        (z_forward(j) if j in (3, 5, 7) else z_copy(j)).wait_send()
        q_copy(j).wait_send()
    for j in range(1, REPLICAS):
        final_copy(j).wait_send()
    for n in range(1, COLUMN):
        seg_copy(n).wait_send()
    for n in range(1, 28):
        part_copy(n).wait_send()
    for n in range(4):
        for j in range(REPLICAS):
            last_copy(n, j).wait_send()


def local(series, tail, queries):
    f32, bf16, dma = jnp.float32, jnp.bfloat16, pltpu.SemaphoreType.DMA
    vmem = pl.BlockSpec(memory_space=pltpu.VMEM)
    prof, qprof = pl.pallas_call(
        kernel,
        out_shape=[jax.ShapeDtypeStruct((32, LANES), f32), jax.ShapeDtypeStruct((1, 32), f32)],
        in_specs=[pl.BlockSpec(memory_space=pl.ANY)] * 3,
        out_specs=[vmem] * 2,
        scratch_shapes=[
            pltpu.VMEM((40, LANES), f32),
            pltpu.VMEM((M - 1,), f32),
            pltpu.VMEM((32, M), f32),
            pltpu.VMEM((COLUMN, 24, LANES), f32),
            pltpu.VMEM((2, LANES, 1280), bf16),
            pltpu.VMEM((2, LANES, 1280), bf16),
            pltpu.VMEM((2, LANES, 1280), bf16),
            pltpu.VMEM((2, LANES, 1280), bf16),
            pltpu.VMEM((GROUP, 72, LANES), f32),
            pltpu.VMEM((256, 896), bf16),
            pltpu.VMEM((256, LANES), f32),
            pltpu.VMEM((COLUMN, 8, LANES), f32),
            pltpu.VMEM((COLUMN, 8, LANES), f32),
            pltpu.VMEM((8, LANES), f32),
            pltpu.VMEM((2, 8, LANES), f32),
            pltpu.VMEM((GROUP, 8, LANES), f32),
            pltpu.VMEM((REPLICAS, 8, LANES), f32),
            pltpu.VMEM((4 * REPLICAS, 8, LANES), f32),
            dma((3,)), dma((1,)), dma((1,)),
            dma((GROUP,)), dma((GROUP,)),
            dma((COLUMN,)), dma((COLUMN,)),
            dma((COLUMN,)), dma((COLUMN,)),
            dma((GROUP,)), dma((GROUP,)),
            dma((20,)), dma((20,)),
        ],
        compiler_params=pltpu.CompilerParams(
            collective_id=0, has_side_effects=True, vmem_limit_bytes=60 * 2**20
        ),
    )(series.reshape(32, LANES), tail, queries)
    return prof.reshape(4096), qprof.reshape(32)


def solution(mesh):
    return jax.shard_map(
        local,
        mesh=mesh,
        in_specs=(P("tm"), P(), P(("tm", "query"), None)),
        out_specs=(P("tm"), P(("tm", "query"))),
        check_vma=False,
    )
```

time: 53.3 us -> 46.8 us (0.88)
  Pallas kernels: 49.1 us -> 44.2 us
  local copies, waits for them, and re-layouts: 3.32 us -> 1.84 us
    pallas_call x1, Pallas kernels: 49.1 us -> 44.2 us  [local(): pl.pallas_call(kernel, out_shape=[jax.ShapeDtypeStruct((32, LANES), f32),...]
    unnamed x6 -> x4, local copies, waits for them, and re-layouts: 2.63 us -> 1.84 us
    reshape x1 -> x0, local copies, waits for them, and re-layouts: 0.69 us -> none  [local(): jnp.pad(tail, (0, 1024 - tail.shape[0])).reshape(8, LANES)]
where the time goes in v2:
time: 46.8 us; the launch traced here: 46.7 us
  Pallas kernels  44.2 us (94%)
  local copies, waits for them, and re-layouts  1.84 us (4%)
  between operations  0.65 us (1%)
    pallas_call x1, Pallas kernels, local(): pl.pallas_call(kernel, out_shape=[jax.ShapeDtypeStruct((32, LANES), f32),...  44.2 us
    unnamed x4, local copies, waits for them, and re-layouts  1.84 us

profile of v2, /device:TPU:1, one launch (start us, length us, event | category | flops | bytes accessed | tf_op | source)
XLA Modules:
  0.0 46.7 jit_solution(14253521236183428555)
XLA Ops:
  0.6 44.2 %shard_map.50 = (f32[32,128]{1,0:T(8,128)}, f32[1,32]{1,0:T(1,128)}) custom-call(f32[32,128]{1,0:T(8,128)} %bitcast.4, f32[287]{0:T(512)} %tail.1, f32[32,288]{1,0:T(8,128)} %queries.1), custom_call_target="tpu_custom_call" | custom-call | tf_op jit(solution)/shard_map/pallas_call | solution.py:350
  44.8 0.0 copy-start
  44.8 1.3 %copy.7 = f32[4096]{0:T(1024)} copy(f32[4096]{0:T(1024)} %bitcast.3) | data formatting | bytes 32768
  46.2 0.0 copy-done
  46.2 0.5 %copy.8 = f32[32]{0:T(128)} copy(f32[32]{0:T(128)S(1)} %bitcast.5) | data formatting | bytes 256
Async XLA Ops:
  44.8 1.3 %copy-start = (f32[1,32]{1,0:T(1,128)S(1)}, f32[1,32]{1,0:T(1,128)}, u32[]{:S(2)}) copy-start(f32[1,32]{1,0:T(1,128)} %get-tuple-element.5) | copy-start | bytes 388

commit v3 on v2

--- a/solution.py
+++ b/solution.py
@@ -63,19 +63,24 @@
     zz, yy, xh = lax.div(tm, 8), lax.rem(lax.div(tm, 2), 4), lax.rem(tm, 2)
     xx, core = xh * 2 + lax.div(q, 2), lax.rem(q, 2)
 
+    z_at = [lax.rem(zz + n, 8) * 8 for n in range(8)]
+    y_at = [lax.rem(yy + n, 4) * 2 + xh for n in range(4)]
+    x_at = [lax.rem(xx + n, 4) for n in range(4)]
+    g_at = [tm - xh + lax.div(x, 2) for x in x_at]
+    q_at = [[lax.rem(x, 2) * 2 + c for c in (core, 1 - core)] for x in x_at]
+    r_at = [lax.rem(q + n, 4) for n in range(4)]
+
     def col(s, sign):
-        s = jnp.int32(s)
-        z2 = lax.rem(zz + sign * lax.div(s, 4) + 8, 8)
-        y2 = lax.rem(yy + sign * lax.rem(s, 4) + 4, 4)
-        return (z2 * 8 + y2 * 2 + xh, q)
+        return (z_at[sign * (s // 4) % 8] + y_at[sign * (s % 4) % 4], q)
+
+    def place(b, n):
+        return (lax.rem(zz - b + 8, 8) * 8 + y_at[-n % 4], q)
 
     def grp(j, sign):
-        x2 = lax.rem(xx + sign * lax.div(j, 2) + 4, 4)
-        c2 = lax.rem(core + lax.rem(j, 2), 2)
-        return (tm - xh + lax.div(x2, 2), lax.rem(x2, 2) * 2 + c2)
+        return (g_at[sign * (j // 2) % 4], q_at[sign * (j // 2) % 4][j % 2])
 
     def rep(j, sign):
-        return (tm, lax.rem(q + sign * j + 4, 4))
+        return (tm, r_at[sign * j % 4])
 
     def remote(src, dst, send, recv, device):
         return pltpu.make_async_remote_copy(
@@ -86,26 +91,27 @@
         return remote(ext.at[0:8], ext.at[32:40], halo_s.at[0], halo_r.at[0], (lax.rem(tm + 63, 64), 3))
 
     def z_copy(j):
-        return remote(zall.at[0], zall.at[j], zs.at[j], zr.at[j], grp(jnp.int32(j), 1))
+        return remote(zall.at[0], zall.at[j], zs.at[j], zr.at[j], grp(j, 1))
 
     def z_forward(j):
-        return remote(zall.at[j - 1], zall.at[j], zs.at[j], zr.at[j], grp(jnp.int32(1), 1))
+        return remote(zall.at[j - 1], zall.at[j], zs.at[j], zr.at[j], grp(1, 1))
 
     def seg_copy(s):
-        return remote(segs.at[0], segs.at[s], ss.at[s], sr.at[s], col(s, 1))
-
-    def part_copy(s):
-        return remote(part.at[s], got.at[s], ps.at[s], pr.at[s], col(s, -1))
+        device = col(s, 1) if isinstance(s, int) else (tm, q)
+        return remote(segs.at[0], segs.at[s], ss.at[s], sr.at[s], device)
+
+    def part_copy(s, device=None):
+        return remote(part.at[s], got.at[s], ps.at[s], pr.at[s], device or col(s, -1))
 
     def q_copy(j):
-        return remote(qpart.at[j % 2], qgot.at[j], qs.at[j], qr.at[j], grp(jnp.int32(j), -1))
+        return remote(qpart.at[j % 2], qgot.at[j], qs.at[j], qr.at[j], grp(j, -1))
 
     def last_copy(n, j):
-        device = (col(28 + n, -1)[0], lax.rem(q + j, 4))
+        device = (col(28 + n, -1)[0], r_at[j])
         return remote(part.at[28 + n], last.at[4 * j + n], fs.at[4 * j + n], fr.at[4 * j + n], device)
 
     def final_copy(j):
-        return remote(pall.at[0], pall.at[j], fs.at[16 + j], fr.at[16 + j], rep(jnp.int32(j), 1))
+        return remote(pall.at[0], pall.at[j], fs.at[16 + j], fr.at[16 + j], rep(j, 1))
 
     def each(low, high, do):
         lax.fori_loop(low, high, lambda i, c: (do(i), c)[1], 0)
@@ -123,10 +129,14 @@
     def hello(device):
         pl.semaphore_signal(barrier, inc=1, device_id=device, device_id_type=MESH)
 
-    each(1, GROUP, lambda j: hello(grp(j, 1)))
-    each(1, COLUMN, lambda s: hello(col(s, 1)))
-    hello((lax.rem(tm + 1, 64), lax.rem(q + 2, 4)))
-    each(0, 12, lambda i: hello((col(28 + lax.rem(i, 4), 1)[0], lax.rem(q + 1 + lax.div(i, 4), 4))))
+    for j in range(1, GROUP):
+        hello(grp(j, 1))
+    for s in range(1, COLUMN):
+        hello(col(s, 1))
+    hello((lax.rem(tm + 1, 64), r_at[2]))
+    for j in range(1, REPLICAS):
+        for n in range(4):
+            hello((col(28 + n, 1)[0], r_at[j]))
 
     loads[0].wait()
     rows = rows_v[...]
@@ -136,8 +146,8 @@
     k = lax.broadcasted_iota(jnp.int32, (M, 384), 0)
     c = lax.broadcasted_iota(jnp.int32, (M, 384), 1)
     source = jnp.where(c < 128, 127 - c, jnp.where(c < 256, 383 - c, 287 - c % REST))
-    place = (k == source).astype(jnp.float32)
-    zp = jnp.dot(zq, place, precision=lax.Precision.HIGHEST, preferred_element_type=jnp.float32)
+    order = (k == source).astype(jnp.bfloat16)
+    zp = sum(jnp.dot(piece, order, preferred_element_type=jnp.float32) for piece in split(zq))
     lane = lax.broadcasted_iota(jnp.int32, (8, LANES), 1)
     quad = lane // REST
     packed = zp[24:32, 256:384]
@@ -146,7 +156,6 @@
     zall[0, 0:32] = zp[:, :128]
     zall[0, 32:64] = zp[:, 128:256]
     zall[0, 64:72] = packed
-    acc[...] = jnp.full_like(acc, -1e30)
     loads[1].wait()
     loads[2].wait()
 
@@ -179,9 +188,13 @@
     @pl.when((q == 3) & (tm < 63))
     def _():
         halo_copy().wait_recv()
+
+    @pl.when((q == 3) & (tm < 63))
+    def _():
         message()
-
-    each(1, COLUMN, lambda s: seg_copy(s).start())
+    for s in range(1, COLUMN):
+        seg_copy(s).start()
+    acc[...] = jnp.full_like(acc, -1e30)
 
     def build(s, bh, bl, i):
         for u, block in hankel(lambda n: segs[s, n : n + 1], 10):
@@ -234,8 +247,6 @@
         zcat[at, 768:896] = mixed.astype(jnp.bfloat16)
 
     def four(s, last=False):
-        for n in (2, 3) if last else (2, 3, 4, 5):
-            seg_copy(s + n).wait_recv()
         compute(s, bha, bla, 0)
         build(s + 2, bhb, blb, 0)
         compute(s + 1, bha, bla, 1)
@@ -246,12 +257,6 @@
         compute(s + 3, bhb, blb, 1)
         if not last:
             build(s + 5, bha, bla, 1)
-        for n in range(4):
-            if last:
-                for j in range(REPLICAS):
-                    last_copy(n, j).start()
-            else:
-                part_copy(s + n).start()
 
     def fold(s):
         part_copy(s).wait_recv()
@@ -288,13 +293,21 @@
 
     def step(i, carry):
         s = 8 * i + 4
-        four(s)
-        four(s + 4)
-
+        for h in (0, 4):
+            for n in range(2, 6):
+                seg_copy(s + h + n).wait_recv()
+            four(s + h)
+            for n in range(4):
+                part_copy(s + h + n, place(2 * i + 1 + h // 4, n)).start()
         return carry
 
     lax.fori_loop(0, 3, step, 0)
+    for n in (30, 31):
+        seg_copy(n).wait_recv()
     four(28, last=True)
+    for n in range(4):
+        for j in range(REPLICAS):
+            last_copy(n, j).start()
 
     best = jnp.max(jnp.transpose(acc[...]), axis=0, keepdims=True)
     qpart[0] = jnp.broadcast_to(best[:, :LANES], (8, LANES))

time: 46.8 us -> 46.5 us (level)
  no operation moved by 1% of the time
where the time goes in v3:
time: 46.5 us; the launch traced here: 46.3 us
  Pallas kernels  43.8 us (94%)
  local copies, waits for them, and re-layouts  1.84 us (4%)
  between operations  0.65 us (1%)
    pallas_call x1, Pallas kernels, local(): pl.pallas_call(kernel, out_shape=[jax.ShapeDtypeStruct((32, LANES), f32),...  43.8 us
    unnamed x4, local copies, waits for them, and re-layouts  1.84 us

profile of v3, /device:TPU:1, one launch (start us, length us, event | category | flops | bytes accessed | tf_op | source)
XLA Modules:
  0.0 46.3 jit_solution(12481594606483186809)
XLA Ops:
  0.6 43.8 %shard_map.50 = (f32[32,128]{1,0:T(8,128)}, f32[1,32]{1,0:T(1,128)}) custom-call(f32[32,128]{1,0:T(8,128)} %bitcast.4, f32[287]{0:T(512)} %tail.1, f32[32,288]{1,0:T(8,128)} %queries.1), custom_call_target="tpu_custom_call" | custom-call | tf_op jit(solution)/shard_map/pallas_call | solution.py:363
  44.4 0.0 copy-start
  44.4 1.3 %copy.7 = f32[4096]{0:T(1024)} copy(f32[4096]{0:T(1024)} %bitcast.3) | data formatting | bytes 32768
  45.8 0.0 copy-done
  45.8 0.5 %copy.8 = f32[32]{0:T(128)} copy(f32[32]{0:T(128)S(1)} %bitcast.5) | data formatting | bytes 256
Async XLA Ops:
  44.4 1.3 %copy-start = (f32[1,32]{1,0:T(1,128)S(1)}, f32[1,32]{1,0:T(1,128)}, u32[]{:S(2)}) copy-start(f32[1,32]{1,0:T(1,128)} %get-tuple-element.5) | copy-start | bytes 388

commit v4 on v3

--- a/solution.py
+++ b/solution.py
@@ -324,6 +324,13 @@
     for j in range(1, REPLICAS):
         final_copy(j).start()
 
+    for j in range(1, GROUP):
+        (z_forward(j) if j in (3, 5, 7) else z_copy(j)).wait_send()
+    for n in range(1, COLUMN):
+        seg_copy(n).wait_send()
+    for n in range(1, 28):
+        part_copy(n).wait_send()
+
     own = qpart[0, 0:1, 0:32]
     for j in range(1, GROUP):
         q_copy(j).wait_recv()
@@ -344,14 +351,9 @@
         halo_copy().wait_send()
 
     for j in range(1, GROUP):
-        (z_forward(j) if j in (3, 5, 7) else z_copy(j)).wait_send()
         q_copy(j).wait_send()
     for j in range(1, REPLICAS):
         final_copy(j).wait_send()
-    for n in range(1, COLUMN):
-        seg_copy(n).wait_send()
-    for n in range(1, 28):
-        part_copy(n).wait_send()
     for n in range(4):
         for j in range(REPLICAS):
             last_copy(n, j).wait_send()

time: 46.5 us -> 46.4 us (level)
  no operation moved by 1% of the time
where the time goes in v4:
time: 46.4 us; the launch traced here: 46.2 us
  Pallas kernels  43.7 us (94%)
  local copies, waits for them, and re-layouts  1.84 us (4%)
  between operations  0.65 us (1%)
    pallas_call x1, Pallas kernels, local(): pl.pallas_call(kernel, out_shape=[jax.ShapeDtypeStruct((32, LANES), f32),...  43.7 us
    unnamed x4, local copies, waits for them, and re-layouts  1.84 us

profile of v4, /device:TPU:1, one launch (start us, length us, event | category | flops | bytes accessed | tf_op | source)
XLA Modules:
  0.0 46.2 jit_solution(15426379532322195089)
XLA Ops:
  0.6 43.7 %shard_map.50 = (f32[32,128]{1,0:T(8,128)}, f32[1,32]{1,0:T(1,128)}) custom-call(f32[32,128]{1,0:T(8,128)} %bitcast.4, f32[287]{0:T(512)} %tail.1, f32[32,288]{1,0:T(8,128)} %queries.1), custom_call_target="tpu_custom_call" | custom-call | tf_op jit(solution)/shard_map/pallas_call | solution.py:365
  44.3 0.0 copy-start
  44.3 1.3 %copy.7 = f32[4096]{0:T(1024)} copy(f32[4096]{0:T(1024)} %bitcast.3) | data formatting | bytes 32768
  45.7 0.0 copy-done
  45.7 0.5 %copy.8 = f32[32]{0:T(128)} copy(f32[32]{0:T(128)S(1)} %bitcast.5) | data formatting | bytes 256
Async XLA Ops:
  44.3 1.3 %copy-start = (f32[1,32]{1,0:T(1,128)S(1)}, f32[1,32]{1,0:T(1,128)}, u32[]{:S(2)}) copy-start(f32[1,32]{1,0:T(1,128)} %get-tuple-element.5) | copy-start | bytes 388

commit v5 on v4

--- a/solution.py
+++ b/solution.py
@@ -269,20 +269,20 @@
         z_forward(j + 1).start()
         take(j)
     compute(0, bha, bla, 0, 0, 128)
-    seg_copy(1).wait_recv()
-    build(1, bha, bla, 1)
-    compute(1, bha, bla, 1, 0, 128)
     z_copy(1).wait_recv()
     take(1)
     for j in (3, 7, 5):
         z_forward(j).wait_recv()
         take(j)
-    for n in (2, 3, 4, 5):
+    for n in (1, 2, 3):
         seg_copy(n).wait_recv()
+    build(1, bha, bla, 1)
     compute(0, bha, bla, 0, 128, 256)
     build(2, bhb, blb, 0)
-    compute(1, bha, bla, 1, 128, 256)
+    compute(1, bha, bla, 1)
     build(3, bhb, blb, 1)
+    for n in (4, 5):
+        seg_copy(n).wait_recv()
     compute(2, bhb, blb, 0)
     build(4, bha, bla, 0)
     compute(3, bhb, blb, 1)

time: 46.4 us -> 46.2 us (level)
  no operation moved by 1% of the time
where the time goes in v5:
time: 46.2 us; the launch traced here: 46.1 us
  Pallas kernels  43.6 us (94%)
  local copies, waits for them, and re-layouts  1.84 us (4%)
  between operations  0.65 us (1%)
    pallas_call x1, Pallas kernels, local(): pl.pallas_call(kernel, out_shape=[jax.ShapeDtypeStruct((32, LANES), f32),...  43.6 us
    unnamed x4, local copies, waits for them, and re-layouts  1.84 us

profile of v5, /device:TPU:1, one launch (start us, length us, event | category | flops | bytes accessed | tf_op | source)
XLA Modules:
  0.0 46.1 jit_solution(3680502123399485077)
XLA Ops:
  0.6 43.6 %shard_map.50 = (f32[32,128]{1,0:T(8,128)}, f32[1,32]{1,0:T(1,128)}) custom-call(f32[32,128]{1,0:T(8,128)} %bitcast.4, f32[287]{0:T(512)} %tail.1, f32[32,288]{1,0:T(8,128)} %queries.1), custom_call_target="tpu_custom_call" | custom-call | tf_op jit(solution)/shard_map/pallas_call | solution.py:365
  44.2 0.0 copy-start
  44.2 1.3 %copy.7 = f32[4096]{0:T(1024)} copy(f32[4096]{0:T(1024)} %bitcast.3) | data formatting | bytes 32768
  45.5 0.0 copy-done
  45.5 0.5 %copy.8 = f32[32]{0:T(128)} copy(f32[32]{0:T(128)S(1)} %bitcast.5) | data formatting | bytes 256
Async XLA Ops:
  44.2 1.3 %copy-start = (f32[1,32]{1,0:T(1,128)S(1)}, f32[1,32]{1,0:T(1,128)}, u32[]{:S(2)}) copy-start(f32[1,32]{1,0:T(1,128)} %get-tuple-element.5) | copy-start | bytes 388
